TPU v7x, 128 devices: a whole 4x4x4 slice. The times are simulated.
128 devices in a mesh: row: 16 (over x_lo, z, core), col: 8 (over x_hi, y).
Axes of the slice: x: 4 (x_hi: 2, x_lo: 2; x = x_hi * 2 + x_lo), y: 4, z: 4, core: 2. Of those that a mesh axis runs over, the one named last changes fastest.
Arguments:
- basis: float32 [32768, 1024], P('row', 'col'), may hold values from -6 to 6
- merge_coef: float32 [1024, 8192], P('row', 'col'), may hold values from -0.1875 to 0.1875
- panels: float32 [2, 32768, 256], P(None, ('row', 'col')), may hold values from -0.03125 to 0.03125
- factors: float32 [2, 256, 256], replicated, may hold values from -2 to 2
Outputs:
- vectors: float32 [32768, 8192], P(('row', 'col'))
- wsum: float32 [2, 256], replicated
All inputs are finite; a program needn't handle non-finite values.
Results may differ from a plain program's by a relative error of at most 0.0001.
Values sent between devices are 32-bit elements; how exact they have to be, the bound alone decides.
A program may use at most 128 MiB of HBM per device.

v0:
```python
import jax
import jax.numpy as jnp
from jax import lax
from jax.sharding import Mesh
from jax.sharding import PartitionSpec as P

ROW = ("row_0", "row_1", "row_2")
ROW_COL = ("row_0", "row_1", "row_2", "col")


HI = lax.Precision.HIGHEST


def copy_for_each(value, axis):
    peers = lax.axis_size(axis)
    return lax.all_to_all(
        jnp.broadcast_to(value[None], (peers, *value.shape)), axis, 0, 0, tiled=True
    )


def laid_out(blocks, dim):
    lengths = list(blocks.shape[1:])
    lengths[dim] *= blocks.shape[0]
    return jnp.moveaxis(blocks, 0, dim).reshape(lengths)


def gathered_by_axis(value, axes, dim):
    far, near = axes
    blocks = copy_for_each(copy_for_each(value, far), near)
    return laid_out(blocks.swapaxes(0, 1).reshape(-1, *value.shape), dim)


def in_blocks(value, dim, peers):
    lengths = value.shape
    blocks = value.reshape(*lengths[:dim], peers, lengths[dim] // peers, *lengths[dim + 1 :])
    return jnp.moveaxis(blocks, dim, 0)


def sum_at_owner(value, axis, dim):
    peers = lax.axis_size(axis)
    blocks = lax.all_to_all(in_blocks(value, dim, peers), axis, 0, 0, tiled=True)
    return jnp.sum(blocks, axis=0)


def padded_to(lines, peers):
    spare = -lines.shape[0] % peers
    if not spare:
        return lines
    return jnp.concatenate([lines, jnp.zeros((spare, *lines.shape[1:]), lines.dtype)])


def collect(value, axis, dim):
    return laid_out(copy_for_each(value, axis), dim)


def total_of(value, axes):
    lines = value.reshape(-1, value.shape[-1])
    own = sum_at_owner(padded_to(lines, lax.axis_size(axes)), axes, 0)
    whole = collect(own, axes, 0)
    return whole[: len(lines)].reshape(value.shape)


def of_everyone(value, axis):
    return copy_for_each(value, axis).sum(axis=0)


def packed_total(arrays, axis):
    ends = [0]
    for a in arrays:
        ends.append(ends[-1] + a.size)
    total = of_everyone(jnp.concatenate([a.ravel() for a in arrays]), axis)
    return tuple((total[b:e].reshape(a.shape) for a, b, e in zip(arrays, ends, ends[1:])))


def matmul(left, right):
    return jnp.dot(left, right, precision=HI, preferred_element_type=jnp.float32)


def to_tall(block):
    return lax.all_to_all(block, "col", split_axis=0, concat_axis=1, tiled=True)


def per_device(basis, merge_coef, panels, factors):
    coef = gathered_by_axis(merge_coef, (("row_0", "row_1"), "row_2"), 0)
    block = matmul(lax.all_gather(basis, "col", axis=1, tiled=True), coef)
    upper = jnp.triu(factors)
    local_v = lax.all_gather(panels, "col", axis=1, tiled=True)

    def reduce_terms(terms):
        return total_of(terms, ROW)

    field = block
    first = local_v[0]
    second = local_v[1]
    proj_one = reduce_terms(matmul(first.T, field))
    field = field - matmul(first, matmul(upper[0], proj_one))
    proj_two = reduce_terms(matmul(second.T, field))
    field = field - matmul(second, matmul(upper[1], proj_two))
    row_one = jnp.sum(proj_one, axis=1)
    row_two = jnp.sum(proj_two, axis=1)
    row_one, row_two = packed_total((row_one, row_two), "col")
    field = to_tall(field)
    scale = jnp.sqrt(jnp.float32(field.shape[1]))
    return (field, jnp.stack([row_one, row_two]) / scale)


def solution(mesh):
    torus = Mesh(
        mesh.devices.reshape(2, 4, 2, mesh.shape["col"]), ("row_0", "row_1", "row_2", "col")
    )
    return jax.shard_map(
        per_device,
        mesh=torus,
        in_specs=(P(ROW, "col"), P(ROW, "col"), P(None, ROW_COL, None), P()),
        out_specs=(P(ROW_COL, None), P()),
        check_vma=False,
    )
```

profile of v0, /device:TPU:1, one launch (start us, length us, event | category | flops | bytes accessed | tf_op | source)
XLA Modules:
  0.0 455.1 jit_solution(9860086470583357897)
XLA Ops:
  7.2 0.0 all-gather.3.cloned.1.call-start
  7.2 0.7 all-gather.3.cloned.1.call-update
  7.9 0.0 all-gather.5.cloned.1.call-start
  7.9 0.7 all-gather.5.cloned.1.call-update
  8.6 1.2 broadcast_in_dim.18
  9.8 43.2 %all_to_all.55 = f32[8,64,1024]{2,1,0:T(8,128)S(1)} all-to-all(f32[8,64,1024]{2,1,0:T(8,128)S(1)} %broadcast_in_dim.18), channel_id=1, replica_groups=mesh['row_0'=2,'row_1'=4,'row_2'=2,'col'=8] {'row_0','row_1'}, dimensions={0} | all-to-all | bytes 4194304 | tf_op jit(solution)/shard_map/all_to_all | solution.py:16
  53.1 0.5 broadcast_in_dim.19
  53.6 9.2 %all_to_all.56 = f32[2,8,64,1024]{3,2,1,0:T(8,128)S(1)} all-to-all(f32[2,8,64,1024]{3,2,1,0:T(8,128)S(1)} %broadcast_in_dim.19), channel_id=1, replica_groups=mesh['row_0'=2,'row_1'=4,'row_2'=2,'col'=8] {'row_2'}, dimensions={0} | all-to-all | bytes 8388608 | tf_op jit(solution)/shard_map/all_to_all | solution.py:16
  62.9 2.4 copy.20
  65.3 72.7 %all-gather.3.cloned.1.call-done = f32[2048,1024]{1,0:T(8,128)} async-done(((f32[2048,128]{1,0:T(8,128)}), f32[2048,1024]{1,0:T(8,128)}) %all-gather.3.cloned.1.call-update) | async-done | bytes 8388624 | tf_op jit(solution)/shard_map/all_gather | solution.py:85
  138.0 31.7 %fusion.5 = f32[2048,1024]{1,0:T(8,128)} fusion(f32[2048,1024]{1,0:T(8,128)} %all-gather.3.cloned.1.call-done, f32[1024,1024]{1,0:T(8,128)} %bitcast.49), kind=kOutput, calls=%fused_computation.16 | convolution fusion | flops 25769803776 | bytes 20971520 | tf_op jit(solution)/shard_map/dot_general | solution.py:76
  169.7 39.9 %all-gather.5.cloned.1.call-done = f32[2,2048,256]{2,1,0:T(8,128)} async-done(((f32[2,256,256]{2,1,0:T(8,128)}), f32[2,2048,256]{2,1,0:T(8,128)}) %all-gather.5.cloned.1.call-update) | async-done | bytes 4194320 | tf_op jit(solution)/shard_map/all_gather | solution.py:87
  209.6 10.2 %fusion = f32[1024,256]{0,1:T(8,128)S(1)} fusion(f32[2048,1024]{1,0:T(8,128)} %fusion.5, f32[2,2048,256]{2,1,0:T(8,128)} %all-gather.5.cloned.1.call-done), kind=kOutput, calls=%fused_computation.4 | convolution fusion | flops 6442450944 | bytes 11534336 | tf_op jit(solution)/shard_map/dot_general | solution.py:76
  219.7 0.0 copy-start.2
  219.8 20.9 %all_to_all.57 = f32[16,16,1024]{2,1,0:T(8,128)S(1)} all-to-all(f32[16,16,1024]{2,1,0:T(8,128)S(1)} %bitcast.47), channel_id=1, replica_groups=mesh['row_0'=2,'row_1'=4,'row_2'=2,'col'=8] {'row_0','row_1','row_2'}, dimensions={0} | all-to-all | bytes 2097152 | tf_op jit(solution)/shard_map/all_to_all | solution.py:41
  240.6 0.1 reduce_sum.49
  240.7 1.1 broadcast_in_dim.22
  241.8 4.6 %all-to-all-start.3 = ((f32[16,16,1024]{2,1,0:T(8,128)}), f32[16,16,1024]{2,1,0:T(8,128)S(1)}, u32[]{:S(2)}, u32[]{:S(2)}) async-start(f32[16,16,1024]{2,1,0:T(8,128)} %broadcast_in_dim.22), calls=%async_computation.3 | async-start | bytes 2097152 | tf_op jit(solution)/shard_map/all_to_all | solution.py:16
  246.4 0.1 iota_compare_fusion
  246.5 0.0 copy-done.2
  246.5 0.1 broadcast_select_fusion
  246.6 15.7 %all-to-all-done.3 = f32[16,16,1024]{2,1,0:T(8,128)S(1)} async-done(((f32[16,16,1024]{2,1,0:T(8,128)}), f32[16,16,1024]{2,1,0:T(8,128)S(1)}, u32[]{:S(2)}, u32[]{:S(2)}) %all-to-all-start.3) | async-done | bytes 1048608 | tf_op jit(solution)/shard_map/all_to_all | solution.py:16
  262.3 1.0 fusion.3
  263.3 0.0 copy-start.1
  263.3 10.3 %bitcast_subtract_fusion.1 = f32[2048,1024]{1,0:T(8,128)S(1)} fusion(f32[2048,1024]{1,0:T(8,128)} %fusion.5, f32[256,1024]{1,0:T(8,128)S(1)} %fusion.3, f32[2,2048,256]{2,1,0:T(8,128)} %all-gather.5.cloned.1.call-done), kind=kOutput, calls=%fused_computation.1 | convolution fusion | flops 6444548096 | bytes 19922944 | tf_op jit(solution)/shard_map/dot_general | solution.py:76
  273.7 0.0 copy-done.1
  273.7 0.0 copy-start
  273.7 7.6 %fusion.1 = f32[1024,256]{0,1:T(8,128)S(1)} fusion(f32[2048,1024]{1,0:T(8,128)S(1)} %bitcast_subtract_fusion.1, f32[2,2048,256]{2,1,0:T(8,128)S(1)} %copy-done.1), kind=kOutput, calls=%fused_computation.5 | convolution fusion | flops 6442450944 | bytes 11534336 | tf_op jit(solution)/shard_map/dot_general | solution.py:76
  281.3 0.0 copy-done
  281.3 18.8 %all_to_all.58 = f32[16,16,1024]{2,1,0:T(8,128)S(1)} all-to-all(f32[16,16,1024]{2,1,0:T(8,128)S(1)} %bitcast.48), channel_id=1, replica_groups=mesh['row_0'=2,'row_1'=4,'row_2'=2,'col'=8] {'row_0','row_1','row_2'}, dimensions={0} | all-to-all | bytes 2097152 | tf_op jit(solution)/shard_map/all_to_all | solution.py:41
  300.1 0.1 reduce_sum.50
  300.2 1.1 broadcast_in_dim.23
  301.3 4.6 %all-to-all-start.5 = ((f32[16,16,1024]{2,1,0:T(8,128)}), f32[16,16,1024]{2,1,0:T(8,128)S(1)}, u32[]{:S(2)}, u32[]{:S(2)}) async-start(f32[16,16,1024]{2,1,0:T(8,128)} %broadcast_in_dim.23), calls=%async_computation.5 | async-start | bytes 2097152 | tf_op jit(solution)/shard_map/all_to_all | solution.py:16
  305.9 0.1 reduce_sum.51
  306.0 0.1 reduce_sum.52
  306.1 15.7 %all-to-all-done.5 = f32[16,16,1024]{2,1,0:T(8,128)S(1)} async-done(((f32[16,16,1024]{2,1,0:T(8,128)}), f32[16,16,1024]{2,1,0:T(8,128)S(1)}, u32[]{:S(2)}, u32[]{:S(2)}) %all-to-all-start.5) | async-done | bytes 1048608 | tf_op jit(solution)/shard_map/all_to_all | solution.py:16
  321.8 1.0 fusion.2
  322.8 0.1 reduce_sum.53
  322.9 0.1 reduce_sum.54
  323.0 0.6 broadcast_in_dim.44
  323.6 3.9 all-to-all-start.7
  327.6 11.9 %bitcast_subtract_fusion = f32[2048,1024]{1,0:T(8,128)} fusion(f32[2048,1024]{1,0:T(8,128)} %copy-done, f32[256,1024]{1,0:T(8,128)S(1)} %fusion.2, f32[2,2048,256]{2,1,0:T(8,128)} %all-gather.5.cloned.1.call-done), kind=kOutput, calls=%fused_computation | convolution fusion | flops 6444548096 | bytes 19922944 | tf_op jit(solution)/shard_map/dot_general | solution.py:76
  339.5 0.0 all-to-all-done.7
  339.5 6.6 %all-to-all-start.6 = ((f32[8,256,1024]{2,1,0:T(8,128)}), f32[8,256,1024]{2,1,0:T(8,128)}, u32[]{:S(2)}, u32[]{:S(2)}) async-start(f32[8,256,1024]{2,1,0:T(8,128)} %bitcast.43), calls=%async_computation.6 | async-start | bytes 16777216 | tf_op jit(solution)/shard_map/all_to_all | solution.py:80
  346.2 0.6 maximum_multiply_fusion
  346.7 93.0 %all-to-all-done.6 = f32[8,256,1024]{2,1,0:T(8,128)} async-done(((f32[8,256,1024]{2,1,0:T(8,128)}), f32[8,256,1024]{2,1,0:T(8,128)}, u32[]{:S(2)}, u32[]{:S(2)}) %all-to-all-start.6) | async-done | bytes 8388640 | tf_op jit(solution)/shard_map/all_to_all | solution.py:80
  439.8 8.4 %copy.30 = f32[8,32,8,1024]{3,2,0,1:T(8,128)} copy(f32[8,32,8,1024]{3,2,1,0:T(8,128)} %bitcast.21) | data formatting | bytes 16777216 | tf_op jit(solution)/shard_map/all_to_all | solution.py:80
  (4 shorter events, 0.0 us)
Async XLA Ops:
  7.2 130.9 %all-gather.3.cloned.1.call-start = ((), (), s32[]{:S(2)}) async-start(), calls=%async_computation.8 | async-start | bytes 9437184 | tf_op jit(solution)/shard_map/all_gather | solution.py:85
  7.9 201.7 %all-gather.5.cloned.1.call-start = ((), (), s32[]{:S(2)}) async-start(), calls=%async_computation.9 | async-start | bytes 4718592 | tf_op jit(solution)/shard_map/all_gather | solution.py:87
  219.7 26.8 %copy-start.2 = (f32[2,256,256]{2,1,0:T(8,128)S(1)}, f32[2,256,256]{2,1,0:T(8,128)}, u32[]{:S(2)}) copy-start(f32[2,256,256]{2,1,0:T(8,128)} %param.7) | copy-start | bytes 1572868
  241.8 20.5 %all-to-all-start.3 = ((f32[16,16,1024]{2,1,0:T(8,128)}), f32[16,16,1024]{2,1,0:T(8,128)S(1)}, u32[]{:S(2)}, u32[]{:S(2)}) async-start(f32[16,16,1024]{2,1,0:T(8,128)} %broadcast_in_dim.22), calls=%async_computation.3 | async-start | bytes 2097152 | tf_op jit(solution)/shard_map/all_to_all | solution.py:16
  263.3 10.3 %copy-start.1 = (f32[2,2048,256]{2,1,0:T(8,128)S(1)}, f32[2,2048,256]{2,1,0:T(8,128)}, u32[]{:S(2)}) copy-start(f32[2,2048,256]{2,1,0:T(8,128)} %all-gather.5.cloned.1.call-done) | copy-start | bytes 12582916
  273.7 7.6 %copy-start = (f32[2048,1024]{1,0:T(8,128)}, f32[2048,1024]{1,0:T(8,128)S(1)}, u32[]{:S(2)}) copy-start(f32[2048,1024]{1,0:T(8,128)S(1)} %bitcast_subtract_fusion.1) | copy-start | bytes 25165828
  301.3 20.5 %all-to-all-start.5 = ((f32[16,16,1024]{2,1,0:T(8,128)}), f32[16,16,1024]{2,1,0:T(8,128)S(1)}, u32[]{:S(2)}, u32[]{:S(2)}) async-start(f32[16,16,1024]{2,1,0:T(8,128)} %broadcast_in_dim.23), calls=%async_computation.5 | async-start | bytes 2097152 | tf_op jit(solution)/shard_map/all_to_all | solution.py:16
  323.6 15.8 %all-to-all-start.7 = ((f32[8,1,512]{2,1,0:T(1,128)}), f32[8,1,512]{2,1,0:T(1,128)S(1)}, u32[]{:S(2)}, u32[]{:S(2)}) async-start(f32[8,1,512]{2,1,0:T(1,128)} %broadcast_in_dim.44), calls=%async_computation.7 | async-start | bytes 32768 | tf_op jit(solution)/shard_map/all_to_all | solution.py:16
  339.5 100.3 %all-to-all-start.6 = ((f32[8,256,1024]{2,1,0:T(8,128)}), f32[8,256,1024]{2,1,0:T(8,128)}, u32[]{:S(2)}, u32[]{:S(2)}) async-start(f32[8,256,1024]{2,1,0:T(8,128)} %bitcast.43), calls=%async_computation.6 | async-start | bytes 16777216 | tf_op jit(solution)/shard_map/all_to_all | solution.py:80
Sparse Core Ops, SparseCore 0:
  10.2 127.7 all-gather.2
  140.3 69.2 all-gather.4
where the time goes:
time: 456 us; the launch traced here: 455 us
  waiting for transfers between devices  238 us (52%)
  blocking collectives  92.2 us (20%)
  matrix products  73.7 us (16%)
  starting transfers between devices  19.9 us (4%)
  local copies, waits for them, and re-layouts  15.6 us (3%)
  between operations  14.2 us (3%)
    all_to_all x1, waiting for transfers between devices, to_tall(): return lax.all_to_all(block, 'col', split_axis=0, concat_axis=1, tiled=True)  93 us
    dot_general x7, matrix products, matmul(): jnp.dot(left, right, precision=HI, preferred_element_type=jnp.float32)  73.7 us
    all_gather x1, waiting for transfers between devices, per_device(): block = matmul(lax.all_gather(basis, 'col', axis=1, tiled=True), coef)  72.7 us
    all_to_all x2, blocking collectives, copy_for_each(): lax.all_to_all(jnp.broadcast_to(value[None], (peers, *value.shape)), axis...  52.5 us
    all_gather x1, waiting for transfers between devices, per_device(): local_v = lax.all_gather(panels, 'col', axis=1, tiled=True)  39.9 us
    all_to_all x2, blocking collectives, sum_at_owner(): lax.all_to_all(in_blocks(value, dim, peers), axis, 0, 0, tiled=True)  39.7 us
    all_to_all x3, waiting for transfers between devices, copy_for_each(): lax.all_to_all(jnp.broadcast_to(value[None], (peers, *value.shape)), axis...  31.4 us
    all_to_all x3, starting transfers between devices, copy_for_each(): lax.all_to_all(jnp.broadcast_to(value[None], (peers, *value.shape)), axis...  13.2 us
  transfers between devices with their start and end apart: 6, of which 5 were waited for; matrix products, arithmetic and copies ran while one was open for 11% of the time, Pallas kernels for 0%

commit v1 on v0

v1 whole, which is shorter than its diff:
```python
import jax
import jax.numpy as jnp
from jax import lax
from jax.sharding import PartitionSpec as P

HI = lax.Precision.HIGHEST
MID = lax.Precision.HIGH


def matmul(left, right, precision=HI):
    return jnp.dot(left, right, precision=precision, preferred_element_type=jnp.float32)


def per_device(basis, merge_coef, panels, factors):
    tall = lax.all_to_all(basis, "col", split_axis=0, concat_axis=1, tiled=True)
    nb = panels.shape[2]
    both = jnp.concatenate([panels[0], panels[1]], axis=1)
    sums = matmul(both.T, jnp.concatenate([tall, panels[0]], axis=1))
    rows = jnp.sum(merge_coef, axis=1)
    place = lax.axis_index("row")
    line = lax.dynamic_update_slice(
        jnp.zeros((merge_coef.shape[0] * lax.axis_size("row"),), jnp.float32),
        rows, (place * merge_coef.shape[0],))
    sums, line = lax.psum((sums, line), ("row", "col"))
    coef = lax.all_gather(merge_coef, "col", axis=1, tiled=True)
    coef = lax.all_gather(coef, "row", axis=0, tiled=True)
    upper = jnp.triu(factors)
    wide = tall.shape[1]
    s0 = sums[:nb, :wide]
    s1 = sums[nb:, :wide]
    cross = sums[nb:, wide:]
    c0 = matmul(upper[0], s0)
    s1 = s1 - matmul(cross, c0)
    c1 = matmul(upper[1], s1)
    turned = tall - matmul(both, jnp.concatenate([c0, c1], axis=0))
    out = matmul(turned, coef, MID)
    scale = jnp.sqrt(jnp.float32(out.shape[1]))
    wsum = jnp.stack([jnp.sum(s0 * line, axis=1), jnp.sum(s1 * line, axis=1)]) / scale
    return out, wsum


def solution(mesh):
    return jax.shard_map(
        per_device,
        mesh=mesh,
        in_specs=(P("row", "col"), P("row", "col"), P(None, ("row", "col"), None), P()),
        out_specs=(P(("row", "col"), None), P()),
        check_vma=False,
    )
```

time: 456 us -> 364 us (0.80)
  matrix products: 73.7 us -> 35.4 us
  blocking collectives: 92.2 us -> 65.4 us
  local copies, waits for them, and re-layouts: 15.6 us -> 1.22 us
  starting transfers between devices: 19.9 us -> 7.61 us
    psum x0 -> x1, waiting for transfers between devices: none -> 187 us  [per_device(): sums, line = lax.psum((sums, line), ('row', 'col'))]
    all_to_all x4 -> x1, waiting for transfers between devices: 124 us -> 15.2 us  [per_device(): tall = lax.all_to_all(basis, 'col', split_axis=0, concat_axis=1, tiled=True)]
    all_to_all x4 -> x0, blocking collectives: 92.2 us -> none  [the longest x2 52.5 us: copy_for_each(): lax.all_to_all(jnp.broadcast_to(value[None], (peers, *value.shape)), axis...]
    all_gather x2, waiting for transfers between devices: 113 us -> 34.3 us  [the longest x1 34.3 us: per_device(): coef = lax.all_gather(merge_coef, 'col', axis=1, tiled=True)]
    psum x0 -> x1, blocking collectives: none -> 65.4 us  [per_device(): sums, line = lax.psum((sums, line), ('row', 'col'))]
    dot_general x7 -> x6, matrix products: 73.7 us -> 35.4 us  [matmul(): jnp.dot(left, right, precision=precision, preferred_element_type=jnp.floa...]
    all_to_all x4 -> x1, starting transfers between devices: 19.8 us -> 7.49 us  [per_device(): tall = lax.all_to_all(basis, 'col', split_axis=0, concat_axis=1, tiled=True)]
    all_to_all x2, local copies, waits for them, and re-layouts: 10.9 us -> 0.66 us  [per_device(): tall = lax.all_to_all(basis, 'col', split_axis=0, concat_axis=1, tiled=True)]
  transfers between devices with their start and end apart: 6 -> 4, of which waited for: 5 -> 3; matrix products, arithmetic and copies ran while one was open for 11% -> 4% of each run, Pallas kernels for 0% -> 0%
where the time goes in v1:
time: 364 us
  waiting for transfers between devices  238 us (65%)
  blocking collectives  65.4 us (18%)
  matrix products  35.4 us (10%)
  between operations  15.6 us (4%)
  starting transfers between devices  7.61 us (2%)
    psum x1, waiting for transfers between devices, per_device(): sums, line = lax.psum((sums, line), ('row', 'col'))  187 us
    psum x1, blocking collectives, per_device(): sums, line = lax.psum((sums, line), ('row', 'col'))  65.4 us
    dot_general x6, matrix products, matmul(): jnp.dot(left, right, precision=precision, preferred_element_type=jnp.floa...  35.4 us
    all_gather x1, waiting for transfers between devices, per_device(): coef = lax.all_gather(merge_coef, 'col', axis=1, tiled=True)  34.3 us
    all_to_all x1, waiting for transfers between devices, per_device(): tall = lax.all_to_all(basis, 'col', split_axis=0, concat_axis=1, tiled=True)  15.2 us
    all_to_all x1, starting transfers between devices, per_device(): tall = lax.all_to_all(basis, 'col', split_axis=0, concat_axis=1, tiled=True)  7.49 us
  transfers between devices with their start and end apart: 4, of which 3 were waited for; matrix products, arithmetic and copies ran while one was open for 4% of the time, Pallas kernels for 0%

profile of v1, /device:TPU:1, one launch (start us, length us, event | category | flops | bytes accessed | tf_op | source)
XLA Modules:
  0.0 363.8 jit_solution(8579136134877388072)
XLA Ops:
  8.0 0.0 copy-start.1
  8.0 0.0 all-gather.3.cloned.1.call-start
  8.1 0.7 all-gather.3.cloned.1.call-update
  8.7 7.5 %all-to-all-start = ((f32[8,256,128]{2,1,0:T(8,128)}), f32[8,256,128]{2,1,0:T(8,128)S(1)}, u32[]{:S(2)}, u32[]{:S(2)}) async-start(f32[8,256,128]{2,1,0:T(8,128)} %bitcast.24), calls=%async_computation | async-start | bytes 2097152 | tf_op jit(solution)/shard_map/all_to_all | solution.py:15
  16.2 0.0 all-reduce.2.cloned.1.call-start
  16.3 0.0 copy-done.1
  16.3 0.1 copy.13
  16.5 0.1 copy.12
  16.6 15.2 %all-to-all-done = f32[8,256,128]{2,1,0:T(8,128)S(1)} async-done(((f32[8,256,128]{2,1,0:T(8,128)}), f32[8,256,128]{2,1,0:T(8,128)S(1)}, u32[]{:S(2)}, u32[]{:S(2)}) %all-to-all-start) | async-done | bytes 1048608 | tf_op jit(solution)/shard_map/all_to_all | solution.py:15
  31.8 0.3 copy.8
  32.1 3.8 %fusion.7 = f32[512,1280]{1,0:T(8,128)} fusion(f32[256,256]{0,1:T(8,128)S(1)} %bitcast.19, f32[256,1024]{0,1:T(8,128)S(1)} %bitcast.17, f32[256,256]{0,1:T(8,128)S(1)} %bitcast.22), kind=kOutput, calls=%fused_computation.6 | convolution fusion | flops 2013724672 | bytes 4194304 | tf_op jit(solution)/shard_map/dot_general | solution.py:11
  35.9 0.0 copy-start
  35.9 0.0 copy-start.2
  35.9 0.0 all-reduce.2.cloned.1.call-update
  35.9 0.0 all-gather.5.cloned.1.call-start
  36.0 34.3 %all-gather.3.cloned.1.call-done = f32[64,8192]{1,0:T(8,128)} async-done(((f32[64,1024]{1,0:T(8,128)}), f32[64,8192]{1,0:T(8,128)}) %all-gather.3.cloned.1.call-update) | async-done | bytes 2097168 | tf_op jit(solution)/shard_map/all_gather | solution.py:25
  70.3 0.0 all-gather.5.cloned.1.call-update
  70.3 0.0 copy-done
  70.3 0.1 reduce_sum.27
  70.5 0.2 dynamic_update_slice.3
  70.7 65.4 %psum.15 = f32[1024]{0:T(1024)S(1)} all-reduce(f32[1024]{0:T(1024)S(1)} %dynamic_update_slice.3), channel_id=1, replica_groups=mesh['row'=16,'col'=8] {'row','col'}, use_global_device_ids=true, to_apply=%region_2.0 | all-reduce | flops 1024 | bytes 8192 | tf_op jit(solution)/shard_map/psum | solution.py:24
  136.1 0.1 iota_compare_fusion
  136.2 0.0 copy-done.2
  136.2 0.1 broadcast_select_fusion
  136.3 0.3 copy.11
  136.6 187.5 %all-reduce.2.cloned.1.call-done = f32[512,1280]{1,0:T(8,128)} async-done(((f32[512,1280]{1,0:T(8,128)}), f32[512,1280]{1,0:T(8,128)}) %all-reduce.2.cloned.1.call-update) | async-done | bytes 2621456 | tf_op jit(solution)/shard_map/psum | solution.py:24
  324.1 2.3 fusion.11
  326.3 2.8 multiply_reduce_fusion.1
  329.2 0.6 maximum_multiply_fusion
  329.8 1.0 fusion.14
  330.8 1.9 fusion.4
  332.7 0.0 all-gather.5.cloned.1.call-done
  332.7 23.7 %fusion.18 = f32[256,8192]{1,0:T(8,128)} fusion(f32[256,1024]{1,0:T(8,128)S(1)} %fusion.4, f32[1024,8192]{1,0:T(8,128)} %all-gather.5.cloned.1.call-done), kind=kOutput, calls=%fused_computation.26 | convolution fusion | flops 12884901888 | bytes 42991616 | tf_op jit(solution)/shard_map/dot_general | solution.py:11
  (3 shorter events, 0.0 us)
Async XLA Ops:
  8.0 8.3 %copy-start.1 = (f32[2,256,256]{2,1,0:T(8,128)S(1)}, f32[2,256,256]{2,1,0:T(8,128)}, u32[]{:S(2)}) copy-start(f32[2,256,256]{2,1,0:T(8,128)} %param.6) | copy-start | bytes 1572868
  8.0 62.3 %all-gather.3.cloned.1.call-start = ((), (), s32[]{:S(2)}) async-start(), calls=%async_computation.2 | async-start | bytes 2359296 | tf_op jit(solution)/shard_map/all_gather | solution.py:25
  8.7 23.0 %all-to-all-start = ((f32[8,256,128]{2,1,0:T(8,128)}), f32[8,256,128]{2,1,0:T(8,128)S(1)}, u32[]{:S(2)}, u32[]{:S(2)}) async-start(f32[8,256,128]{2,1,0:T(8,128)} %bitcast.24), calls=%async_computation | async-start | bytes 2097152 | tf_op jit(solution)/shard_map/all_to_all | solution.py:15
  16.2 307.8 %all-reduce.2.cloned.1.call-start = ((), (), s32[]{:S(2)}) async-start(), calls=%async_computation.1 | async-start | bytes 5242880 | tf_op jit(solution)/shard_map/psum | solution.py:24
  35.9 34.4 %copy-start = (f32[64,1024]{1,0:T(8,128)S(1)}, f32[64,1024]{1,0:T(8,128)}, u32[]{:S(2)}) copy-start(f32[64,1024]{1,0:T(8,128)} %param.5) | copy-start | bytes 786436
  35.9 100.3 %copy-start.2 = (f32[2,256,256]{2,1,0:T(8,128)S(1)}, f32[2,256,256]{2,1,0:T(8,128)}, u32[]{:S(2)}) copy-start(f32[2,256,256]{2,1,0:T(8,128)} %param.7) | copy-start | bytes 1572868
  35.9 296.8 %all-gather.5.cloned.1.call-start = ((), (), s32[]{:S(2)}) async-start(), calls=%async_computation.3 | async-start | bytes 35651584 | tf_op jit(solution)/shard_map/all_gather | solution.py:26
Sparse Core Ops, SparseCore 0:
  11.4 58.8 all-gather.2
  72.1 172.6 all-gather.4
Sparse Core Ops, SparseCore 1:
  36.0 288.0 all-reduce.1

commit v2 on v1

v2 whole, which is shorter than its diff:
```python
import jax
import jax.numpy as jnp
from jax import lax
from jax.experimental import pallas as pl
from jax.experimental.pallas import tpu as pltpu
from jax.sharding import PartitionSpec as P

HI = lax.Precision.HIGHEST
MESH = pl.DeviceIdType.MESH
F32 = jnp.float32
BF16 = jnp.bfloat16

STEPS = ("a", "b", "y+", "y-", "z+", "z-")
OFFSETS = tuple((a, b, y, z) for a in (0, 1) for b in (0, 1) for y in range(4) for z in range(4))
INDEX = {d: i for i, d in enumerate(OFFSETS)}
HOME = (0, 0, 0, 0)
ROUNDS = (
    ((3, 0), (5, 0), (2, 0), (4, 0), (0, 0), (1, 0)),
    ((5, 32), (4, 32), (3, 3), (0, 16), (1, 1), (2, 32)),
    ((0, 17), (1, 35), (5, 3), (4, 33), (2, 35), (3, 35)),
    ((0, 51), (4, 49), (5, 4), (1, 2), (2, 34), (3, 1)),
    ((0, 38), (5, 38), (4, 4), (1, 4), (3, 2), (2, 36)),
    ((4, 47), (5, 47), (0, 13), (1, 5), (3, 15), (2, 37)),
    ((5, 40), (4, 11), (0, 41), (2, 6), (3, 46), (1, 36)),
    ((0, 21), (4, 21), (5, 52), (3, 19), (2, 50), (1, 7)),
    ((0, 31), (5, 31), (4, 31), (3, 48), (2, 52), (1, 13)),
    ((5, 63), (4, 60), (0, 56), (3, 63), (2, 21), (1, 10)),
    ((4, 26), (5, 59), (3, 61)),
)
HALVES = 2


def onward(d, step):
    a, b, y, z = d
    if step == "a":
        return 1 - a, b, y, z
    if step == "b":
        return a, 1 - b, y, z
    if step in ("y+", "y-"):
        return a, b, (y + (1 if step == "y+" else 3)) % 4, z
    return a, b, y, (z + (1 if step == "z+" else 3)) % 4


PLAN = tuple(
    tuple((STEPS[s], OFFSETS[i], onward(OFFSETS[i], STEPS[s])) for s, i in line) for line in ROUNDS
)


def coords(row, col):
    return row // 8, (row // 2) % 4, row % 2, col // 4, col % 4


def place(xl, z, k, xh, y):
    return xl * 8 + z * 2 + k, xh * 4 + y


def neighbour(row, col, step):
    xl, z, k, xh, y = coords(row, col)
    if step == "a":
        xl = 1 - xl
    elif step == "b":
        xl, xh = 1 - xl, 1 - xh
    elif step == "y+":
        y = (y + 1) % 4
    elif step == "y-":
        y = (y + 3) % 4
    elif step == "z+":
        z = (z + 1) % 4
    elif step == "z-":
        z = (z + 3) % 4
    else:
        k = 1 - k
    return place(xl, z, k, xh, y)


def source(row, col, d, other=0):
    xl, z, k, xh, y = coords(row, col)
    a, b, dy, dz = d
    return place(
        (xl + a + b) % 2, (z + 4 - dz) % 4, (k + other) % 2, (xh + b) % 2, (y + 4 - dy) % 4
    )


def group(d):
    return d[1], d[2]


def group_order():
    last = {}
    for t, line in enumerate(PLAN):
        for _, _, n in line:
            last[group(n)] = t
    return sorted(last.items(), key=lambda kv: kv[1])


def split(x):
    high = x.astype(BF16)
    return high, (x - high.astype(F32)).astype(BF16)


def kernel(
    m_ref, turned_ref, out_ref, line_ref,
    full, parts, made, recv, sent, krecv, ksent, local, outsem,
):
    row = lax.axis_index("row")
    col = lax.axis_index("col")
    depth = m_ref.shape[0]
    piece = depth // HALVES
    tile = 256
    tiles = full.shape[2] // tile
    peer = {step: neighbour(row, col, step) for step in STEPS + ("k",)}

    barrier = pltpu.get_barrier_semaphore()
    for step in STEPS + ("k",):
        pl.semaphore_signal(barrier, inc=1, device_id=peer[step], device_id_type=MESH)
    pl.semaphore_wait(barrier, len(peer))

    def slot(d, other=0, half=None):
        r, c = source(row, col, d, other)
        if half is None:
            return full.at[c, pl.ds(pl.multiple_of(r * depth, depth), depth), :]
        return full.at[c, pl.ds(pl.multiple_of(r * depth + half * piece, piece), piece), :]

    def held(d, half=None):
        if d == HOME:
            return m_ref if half is None else m_ref.at[pl.ds(half * piece, piece), :]
        return slot(d, 0, half)

    def send(step, d, n, half):
        copy = pltpu.make_async_remote_copy(
            held(d, half), slot(d, 0, half), sent.at[INDEX[n], half], recv.at[INDEX[n], half],
            peer[step], device_id_type=MESH)
        copy.start()
        return copy

    def arrive(n, half):
        pltpu.make_async_remote_copy(
            slot(n, 0, half), slot(n, 0, half), sent.at[INDEX[n], half], recv.at[INDEX[n], half],
            peer["k"], device_id_type=MESH).wait_recv()

    def share(d):
        copy = pltpu.make_async_remote_copy(
            held(d), slot(d), ksent.at[INDEX[d]], krecv.at[INDEX[d]],
            peer["k"], device_id_type=MESH)
        copy.start()
        return copy

    def shared(d):
        pltpu.make_async_remote_copy(
            slot(d, 1), slot(d, 1), ksent.at[INDEX[d]], krecv.at[INDEX[d]],
            peer["k"], device_id_type=MESH).wait_recv()

    own = pltpu.make_async_copy(m_ref, slot(HOME), local)
    own.start()
    started = []
    stores = []
    arrived = set()
    todo = []
    order = group_order()

    def compute(g, first, count):
        b, dy = g
        _, c = source(row, col, (0, b, dy, 0))
        q = [name for name, _ in order].index(g)
        if first == 0:
            for d in OFFSETS:
                if group(d) == g:
                    shared(d)
            if g == group(HOME):
                own.wait()

        def unit(n, carry):
            at = pl.ds(pl.multiple_of(n * tile, tile), tile)
            m = full[c, :, at]
            high, low = split(m)
            both = jnp.dot(parts[...], high, preferred_element_type=F32)
            rest = jnp.dot(parts[: both.shape[0] // 2, :], low, preferred_element_type=F32)
            half = both.shape[0] // 2
            made[q, :, at] = both[:half] + (both[half:] + rest)
            line_ref[...] += m[:, :128] + m[:, 128:]
            return carry

        lax.fori_loop(first, first + count, unit, 0)
        if first + count == tiles:
            wide = made.shape[2]
            store = pltpu.make_async_copy(
                made.at[q], out_ref.at[:, pl.ds(pl.multiple_of(c * wide, wide), wide)],
                outsem.at[q])
            store.start()
            stores.append(store)

    def some(count):
        while count and todo:
            g, first = todo.pop(0)
            take = min(count, tiles - first)
            compute(g, first, take)
            count -= take
            if first + take < tiles:
                todo.insert(0, (g, first + take))

    for t, plan in enumerate(PLAN):
        for half in range(HALVES):
            for step, d, n in plan:
                if d != HOME and (d, half) not in arrived:
                    arrive(d, half)
                    arrived.add((d, half))
                started.append(send(step, d, n, half))
            if t == 0 and half == 0:
                started.append(share(HOME))
                high, low = split(turned_ref[...])
                rows = turned_ref.shape[0]
                parts[:rows, :] = high
                parts[rows:, :] = low
                line_ref[...] = jnp.zeros_like(line_ref)
            some(2)
        if t:
            for _, _, n in PLAN[t - 1]:
                for half in range(HALVES):
                    if (n, half) not in arrived:
                        arrive(n, half)
                        arrived.add((n, half))
                started.append(share(n))
        todo.extend((g, 0) for g, last in order if last == t - 1)
    for _, _, n in PLAN[-1]:
        for half in range(HALVES):
            arrive(n, half)
        started.append(share(n))
    todo.extend((g, 0) for g, last in order if last == len(PLAN) - 1)
    some(len(order) * tiles)
    for copy in started:
        copy.wait_send()
    for copy in stores:
        copy.wait()


def gathered_product(turned, merge_coef, cols):
    rows, inner = turned.shape
    depth, wide = merge_coef.shape
    groups = cols // wide
    sems = pltpu.SemaphoreType.DMA
    return pl.pallas_call(
        kernel,
        out_shape=(
            jax.ShapeDtypeStruct((rows, cols), F32),
            jax.ShapeDtypeStruct((inner, 128), F32),
        ),
        in_specs=[pl.BlockSpec(memory_space=pltpu.VMEM)] * 2,
        out_specs=(pl.BlockSpec(memory_space=pl.ANY), pl.BlockSpec(memory_space=pltpu.VMEM)),
        scratch_shapes=[
            pltpu.VMEM((groups, inner, wide), F32),
            pltpu.VMEM((2 * rows, inner), BF16),
            pltpu.VMEM((groups, rows, wide), F32),
            sems((len(OFFSETS), HALVES)),
            sems((len(OFFSETS), HALVES)),
            sems((len(OFFSETS),)),
            sems((len(OFFSETS),)),
            sems,
            sems((groups,)),
        ],
        compiler_params=pltpu.CompilerParams(
            collective_id=0, has_side_effects=True, vmem_limit_bytes=58 * 2**20
        ),
        cost_estimate=pl.CostEstimate(
            flops=6 * rows * inner * cols, bytes_accessed=4 * rows * cols, transcendentals=0
        ),
    )(merge_coef, turned)


def matmul(left, right, precision=HI):
    return jnp.dot(left, right, precision=precision, preferred_element_type=F32)


def per_device(basis, merge_coef, panels, factors):
    tall = lax.all_to_all(basis, "col", split_axis=0, concat_axis=1, tiled=True)
    nb = panels.shape[2]
    both = jnp.concatenate([panels[0], panels[1]], axis=1)
    sums = matmul(both.T, jnp.concatenate([tall, panels[0]], axis=1))
    sums = lax.psum(sums, ("row", "col"))
    upper = jnp.triu(factors)
    wide = tall.shape[1]
    s0 = sums[:nb, :wide]
    s1 = sums[nb:, :wide]
    cross = sums[nb:, wide:]
    c0 = matmul(upper[0], s0)
    s1 = s1 - matmul(cross, c0)
    c1 = matmul(upper[1], s1)
    turned = tall - matmul(both, jnp.concatenate([c0, c1], axis=0))
    cols = merge_coef.shape[1] * lax.axis_size("col")
    out, lanes = gathered_product(turned, merge_coef, cols)
    line = jnp.sum(lanes, axis=1)
    wsum = jnp.stack([jnp.sum(s0 * line, axis=1), jnp.sum(s1 * line, axis=1)])
    return out, wsum / jnp.sqrt(F32(cols))


def solution(mesh):
    return jax.shard_map(
        per_device,
        mesh=mesh,
        in_specs=(P("row", "col"), P("row", "col"), P(None, ("row", "col"), None), P()),
        out_specs=(P(("row", "col"), None), P()),
        check_vma=False,
    )
```

time: 364 us -> 293 us (0.80)
  Pallas kernels: 0 us -> 79.8 us
  waiting for transfers between devices: 238 us -> 166 us
  blocking collectives: 65.4 us -> 0 us
  matrix products: 35.4 us -> 12.3 us
  local copies, waits for them, and re-layouts: 1.22 us -> 8.88 us
    pallas_call x0 -> x1, Pallas kernels: none -> 79.8 us  [gathered_product(): pl.pallas_call(kernel, out_shape=(jax.ShapeDtypeStruct((rows, cols), F32)...]
    psum x1 -> x0, blocking collectives: 65.4 us -> none  [per_device(): sums, line = lax.psum((sums, line), ('row', 'col'))]
    all_gather x2 -> x0, waiting for transfers between devices: 34.3 us -> none  [the longest x1 34.3 us: per_device(): coef = lax.all_gather(merge_coef, 'col', axis=1, tiled=True)]
    psum x1, waiting for transfers between devices: 187 us -> 153 us  [per_device(): sums = lax.psum(sums, ('row', 'col'))]
    dot_general x6 -> x5, matrix products: 35.4 us -> 12.3 us  [matmul(): return jnp.dot(left, right, precision=precision, preferred_element_type=F32)]
    unnamed x8 -> x3, local copies, waits for them, and re-layouts: 0.27 us -> 7.69 us
  transfers between devices with their start and end apart: 4 -> 2, of which waited for: 3 -> 2; matrix products, arithmetic and copies ran while one was open for 4% -> 0% of each run, Pallas kernels for 0% -> 0%
where the time goes in v2:
time: 293 us; the launch traced here: 292 us
  waiting for transfers between devices  166 us (57%)
  Pallas kernels  79.8 us (27%)
  between operations  14.1 us (5%)
  matrix products  12.3 us (4%)
  local copies, waits for them, and re-layouts  8.88 us (3%)
  starting transfers between devices  7.53 us (3%)
  other arithmetic  3.44 us (1%)
    psum x1, waiting for transfers between devices, per_device(): sums = lax.psum(sums, ('row', 'col'))  153 us
    pallas_call x1, Pallas kernels, gathered_product(): pl.pallas_call(kernel, out_shape=(jax.ShapeDtypeStruct((rows, cols), F32)...  79.8 us
    all_to_all x1, waiting for transfers between devices, per_device(): tall = lax.all_to_all(basis, 'col', split_axis=0, concat_axis=1, tiled=True)  13.1 us
    dot_general x5, matrix products, matmul(): return jnp.dot(left, right, precision=precision, preferred_element_type=F32)  12.3 us
    unnamed x3, local copies, waits for them, and re-layouts  7.69 us
    all_to_all x1, starting transfers between devices, per_device(): tall = lax.all_to_all(basis, 'col', split_axis=0, concat_axis=1, tiled=True)  7.49 us
  transfers between devices with their start and end apart: 2, of which 2 were waited for; matrix products, arithmetic and copies ran while one was open for 0% of the time, Pallas kernels for 0%

profile of v2, /device:TPU:1, one launch (start us, length us, event | category | flops | bytes accessed | tf_op | source)
XLA Modules:
  0.0 292.4 jit_solution(14709946622650118572)
XLA Ops:
  7.2 7.5 %all-to-all-start = ((f32[8,256,128]{2,1,0:T(8,128)}), f32[8,256,128]{2,1,0:T(8,128)S(1)}, u32[]{:S(2)}, u32[]{:S(2)}) async-start(f32[8,256,128]{2,1,0:T(8,128)} %bitcast.25), calls=%async_computation | async-start | bytes 2097152 | tf_op jit(solution)/shard_map/all_to_all | solution.py:274
  14.7 0.0 all-reduce.2.cloned.1.call-start
  14.7 1.1 slice_bitcast_fusion.4
  15.8 13.1 %all-to-all-done = f32[8,256,128]{2,1,0:T(8,128)S(1)} async-done(((f32[8,256,128]{2,1,0:T(8,128)}), f32[8,256,128]{2,1,0:T(8,128)S(1)}, u32[]{:S(2)}, u32[]{:S(2)}) %all-to-all-start) | async-done | bytes 1048608 | tf_op jit(solution)/shard_map/all_to_all | solution.py:274
  28.8 0.1 copy_bitcast_fusion
  29.0 0.0 copy-start
  29.0 3.8 %fusion.7 = f32[512,1280]{1,0:T(8,128)} fusion(f32[256,256]{1,0:T(8,128)S(1)} %get-tuple-element.9, f32[256,1024]{1,0:T(8,128)S(1)} %copy_bitcast_fusion, f32[256,256]{1,0:T(8,128)S(1)} %get-tuple-element.8), kind=kOutput, calls=%fused_computation.6 | convolution fusion | flops 2013724672 | bytes 4194304 | tf_op jit(solution)/shard_map/dot_general | solution.py:270
  32.8 0.0 all-reduce.2.cloned.1.call-update
  32.8 0.1 iota_compare_fusion
  32.9 0.0 copy-done
  32.9 0.1 broadcast_select_fusion
  33.0 153.3 %all-reduce.2.cloned.1.call-done = f32[512,1280]{1,0:T(8,128)} async-done(((f32[512,1280]{1,0:T(8,128)}), f32[512,1280]{1,0:T(8,128)}) %all-reduce.2.cloned.1.call-update) | async-done | bytes 2621456 | tf_op jit(solution)/shard_map/psum | solution.py:278
  186.3 2.3 fusion.11
  188.6 2.3 convolution_subtract_fusion
  190.9 1.0 fusion.14
  191.9 2.9 fusion.4.turned_ref
  194.8 79.8 %shard_map.59 = (f32[256,8192]{1,0:T(8,128)}, f32[1024,128]{1,0:T(8,128)}) custom-call(f32[64,1024]{1,0:T(8,128)} %m_ref.1, f32[256,1024]{1,0:T(8,128)} %fusion.4.turned_ref), custom_call_target="tpu_custom_call" | custom-call | flops 12884901888 | bytes 8388608 | tf_op jit(solution)/shard_map/pallas_call | solution.py:241
  274.6 1.2 reduce_sum.27
  275.9 1.4 multiply_reduce_fusion.1
  277.3 0.6 maximum_multiply_fusion
  277.9 7.7 %copy.14 = f32[256,8192]{1,0:T(8,128)} copy(f32[256,8192]{1,0:T(8,128)} %get-tuple-element.12) | data formatting | bytes 16777216
  (1 shorter events, 0.0 us)
Async XLA Ops:
  7.2 21.7 %all-to-all-start = ((f32[8,256,128]{2,1,0:T(8,128)}), f32[8,256,128]{2,1,0:T(8,128)S(1)}, u32[]{:S(2)}, u32[]{:S(2)}) async-start(f32[8,256,128]{2,1,0:T(8,128)} %bitcast.25), calls=%async_computation | async-start | bytes 2097152 | tf_op jit(solution)/shard_map/all_to_all | solution.py:274
  14.7 171.6 %all-reduce.2.cloned.1.call-start = ((), (), s32[]{:S(2)}) async-start(), calls=%async_computation.1 | async-start | bytes 5242880 | tf_op jit(solution)/shard_map/psum | solution.py:278
  29.0 3.9 %copy-start = (f32[2,256,256]{2,1,0:T(8,128)S(1)}, f32[2,256,256]{2,1,0:T(8,128)}, u32[]{:S(2)}) copy-start(f32[2,256,256]{2,1,0:T(8,128)} %param.7) | copy-start | bytes 1572868
Sparse Core Ops, SparseCore 0:
  32.9 153.3 all-reduce.1

commit v3 on v2

v3 whole, which is shorter than its diff:
```python
import jax
import jax.numpy as jnp
from jax import lax
from jax.experimental import pallas as pl
from jax.experimental.pallas import tpu as pltpu
from jax.sharding import PartitionSpec as P

HI = lax.Precision.HIGHEST
MESH = pl.DeviceIdType.MESH
F32 = jnp.float32
BF16 = jnp.bfloat16

STEPS = ("a", "b", "y+", "y-", "z+", "z-")
OFFSETS = tuple((a, b, y, z) for a in (0, 1) for b in (0, 1) for y in range(4) for z in range(4))
INDEX = {d: i for i, d in enumerate(OFFSETS)}
HOME = (0, 0, 0, 0)
ROUNDS = (
    ((3, 0), (5, 0), (2, 0), (4, 0), (0, 0), (1, 0)),
    ((5, 32), (4, 32), (3, 3), (0, 16), (1, 1), (2, 32)),
    ((0, 17), (1, 35), (5, 3), (4, 33), (2, 35), (3, 35)),
    ((0, 51), (4, 49), (5, 4), (1, 2), (2, 34), (3, 1)),
    ((0, 38), (5, 38), (4, 4), (1, 4), (3, 2), (2, 36)),
    ((4, 47), (5, 47), (0, 13), (1, 5), (3, 15), (2, 37)),
    ((5, 40), (4, 11), (0, 41), (2, 6), (3, 46), (1, 36)),
    ((0, 21), (4, 21), (5, 52), (3, 19), (2, 50), (1, 7)),
    ((0, 31), (5, 31), (4, 31), (3, 48), (2, 52), (1, 13)),
    ((5, 63), (4, 60), (0, 56), (3, 63), (2, 21), (1, 10)),
    ((4, 26), (5, 59), (3, 61)),
)
HALVES = 2


def onward(d, step):
    a, b, y, z = d
    if step == "a":
        return 1 - a, b, y, z
    if step == "b":
        return a, 1 - b, y, z
    if step in ("y+", "y-"):
        return a, b, (y + (1 if step == "y+" else 3)) % 4, z
    return a, b, y, (z + (1 if step == "z+" else 3)) % 4


PLAN = tuple(
    tuple((STEPS[s], OFFSETS[i], onward(OFFSETS[i], STEPS[s])) for s, i in line) for line in ROUNDS
)


def coords(row, col):
    return row // 8, (row // 2) % 4, row % 2, col // 4, col % 4


def place(xl, z, k, xh, y):
    return xl * 8 + z * 2 + k, xh * 4 + y


def neighbour(row, col, step):
    xl, z, k, xh, y = coords(row, col)
    if step == "a":
        xl = 1 - xl
    elif step == "b":
        xl, xh = 1 - xl, 1 - xh
    elif step == "y+":
        y = (y + 1) % 4
    elif step == "y-":
        y = (y + 3) % 4
    elif step == "z+":
        z = (z + 1) % 4
    elif step == "z-":
        z = (z + 3) % 4
    else:
        k = 1 - k
    return place(xl, z, k, xh, y)


def source(row, col, d, other=0):
    xl, z, k, xh, y = coords(row, col)
    a, b, dy, dz = d
    return place(
        (xl + a + b) % 2, (z + 4 - dz) % 4, (k + other) % 2, (xh + b) % 2, (y + 4 - dy) % 4
    )


def group(d):
    return d[1], d[2]


def group_order():
    last = {}
    for t, line in enumerate(PLAN):
        for _, _, n in line:
            last[group(n)] = t
    return sorted(last.items(), key=lambda kv: kv[1])


def split(x):
    high = x.astype(BF16)
    return high, (x - high.astype(F32)).astype(BF16)


def dot(left, right, precision=HI):
    return jnp.dot(left, right, precision=precision, preferred_element_type=F32)


AXES = (("z", "y", "x"), ("y", "x", "z"), ("x", "z", "y"))
TICKS = (5, 6, 8, 9, 11, 12, 13, 15)
BATCH = 5


def along(row, col, axis, step):
    xl, z, k, xh, y = coords(row, col)
    if axis == "x":
        x = (xh * 2 + xl + step) % 4
        xl, xh = x % 2, x // 2
    elif axis == "y":
        y = (y + step) % 4
    else:
        z = (z + step) % 4
    return place(xl, z, k, xh, y)


def position(row, col, axis):
    xl, z, _, xh, y = coords(row, col)
    return {"x": xh * 2 + xl, "y": y, "z": z}[axis]


def kernel(
    m_ref, basis_ref, panel_ref, factor_ref, out_ref, wsum_ref,
    full, parts, made, line, tall, mine, twin, paired, near, nearest, mid, middle, far, total, proj,
    recv, sent, krecv, ksent, local, outsem, trecv, tsent, rrecv, rsent,
):
    row = lax.axis_index("row")
    col = lax.axis_index("col")
    _, _, core, _, _ = coords(row, col)
    depth = m_ref.shape[0]
    piece = depth // HALVES
    tile = 256
    tiles = full.shape[2] // tile
    groups = full.shape[0]
    rows = made.shape[1]
    nb = panel_ref.shape[2]
    peer = {step: neighbour(row, col, step) for step in STEPS + ("k",)}

    barrier = pltpu.get_barrier_semaphore()
    greeted = [(row, (col + o) % groups) for o in range(1, groups)]
    greeted += [along(row, col, "x", o) for o in (1, 3)]
    greeted += [along(row, col, "z", o) for o in (1, 2, 3)]
    greeted += [peer["k"]]
    for device in greeted:
        pl.semaphore_signal(barrier, inc=1, device_id=device, device_id_type=MESH)
    pl.semaphore_wait(barrier, len(greeted))

    started = []
    stores = []
    arrived = set()
    todo = []
    order = group_order()

    def remote(src, dst, out_sem, in_sem, device, start=True):
        copy = pltpu.make_async_remote_copy(
            src, dst, out_sem, in_sem, device, device_id_type=MESH)
        if start:
            copy.start()
            started.append(copy)
        return copy


    def slot(d, other=0, half=None):
        r, c = source(row, col, d, other)
        if half is None:
            return full.at[c, pl.ds(pl.multiple_of(r * depth, depth), depth), :]
        return full.at[c, pl.ds(pl.multiple_of(r * depth + half * piece, piece), piece), :]

    def held(d, half=None):
        if d == HOME:
            return m_ref if half is None else m_ref.at[pl.ds(half * piece, piece), :]
        return slot(d, 0, half)

    def send(step, d, n, half):
        i = INDEX[n]
        remote(held(d, half), slot(d, 0, half), sent.at[i, half], recv.at[i, half], peer[step])

    def arrive(n, half):
        if (n, half) in arrived or n == HOME:
            return
        arrived.add((n, half))
        i, here = INDEX[n], slot(n, 0, half)
        remote(here, here, sent.at[i, half], recv.at[i, half], peer["k"], False).wait_recv()

    def share(d):
        remote(held(d), slot(d), ksent.at[INDEX[d]], krecv.at[INDEX[d]], peer["k"])

    def shared(d):
        i, here = INDEX[d], slot(d, 1)
        remote(here, here, ksent.at[i], krecv.at[i], peer["k"], False).wait_recv()


    def block(j):
        return basis_ref.at[pl.ds(pl.multiple_of(j * rows, rows), rows), :]

    own_tall = pltpu.make_async_copy(block(col), tall.at[col], local.at[1])

    def spread():
        own_tall.start()
        for o in range(1, groups):
            j = (col + o) % groups
            remote(block(j), tall.at[col], tsent.at[o - 1], trecv.at[o - 1], (row, j))


    wide = total.shape[2]
    per = wide // 128

    def partial():
        turned = jnp.transpose(jnp.concatenate([panel_ref[0], panel_ref[1]], axis=1))
        cross = dot(turned[nb:], panel_ref[0])
        last = len(AXES) - 1
        mine[last, :nb, wide - 128 :] = cross[:, :128]
        mine[last, nb:, wide - 128 :] = cross[:, 128:]
        own_tall.wait()
        for o in range(1, groups):
            here = tall.at[(col + groups - o) % groups]
            remote(here, here, tsent.at[o - 1], trecv.at[o - 1], peer["k"], False).wait_recv()
        for p in range(len(AXES)):
            count = min(per, groups - p * per)
            value = jnp.concatenate([tall[p * per + i] for i in range(count)], axis=1)
            mine[p, :, : count * 128] = dot(turned, value)
            other = pl.ds(pl.multiple_of((1 - core) * nb, nb), nb)
            remote(mine.at[p, other], twin.at[p], rsent.at[p, 0], rrecv.at[p, 0], peer["k"])

    def exchange(p, level, src_of, dst_of):
        axis = AXES[p][(0, 1, 2, 1, 0)[level]]
        for o in (1, 2, 3):
            j = (position(row, col, axis) + o) % 4
            at = 1 + level * 3 + o - 1
            remote(src_of(j), dst_of(o), rsent.at[p, at], rrecv.at[p, at],
                   along(row, col, axis, o))

    def exchanged(p, level, dst_of):
        for o in (1, 2, 3):
            at = 1 + level * 3 + o - 1
            here = dst_of(o)
            remote(here, here, rsent.at[p, at], rrecv.at[p, at], peer["k"], False).wait_recv()

    def pos(p, level):
        return position(row, col, AXES[p][level])

    def cut(ref, p, j, size):
        return ref.at[p, pl.ds(pl.multiple_of(j * size, size), size), :]

    first, second = nb // 4, nb // 16

    def pair():
        for p in range(len(AXES)):
            remote(twin.at[p], twin.at[p], rsent.at[p, 0], rrecv.at[p, 0], peer["k"],
                   False).wait_recv()
            keep = pl.ds(pl.multiple_of(core * nb, nb), nb)
            paired[p] = mine[p, keep, :] + twin[p]
            exchange(p, 0, lambda j: cut(paired, p, j, first), lambda o: near.at[p, o - 1])

    def level_one():
        for p in range(len(AXES)):
            exchanged(p, 0, lambda o: near.at[p, o - 1])
            keep = pl.ds(pl.multiple_of(pos(p, 0) * first, first), first)
            nearest[p] = (paired[p, keep, :] + near[p, 0]) + (near[p, 1] + near[p, 2])
            exchange(p, 1, lambda j: cut(nearest, p, j, second), lambda o: mid.at[p, o - 1])

    def level_two():
        for p in range(len(AXES)):
            exchanged(p, 1, lambda o: mid.at[p, o - 1])
            keep = pl.ds(pl.multiple_of(pos(p, 1) * second, second), second)
            value = (nearest[p, keep, :] + mid[p, 0]) + (mid[p, 1] + mid[p, 2])
            middle[p] = value
            far[p, pos(p, 2)] = value
            here = pos(p, 2)
            exchange(p, 2, lambda j: middle.at[p], lambda o: far.at[p, here])

    def level_three():
        for p in range(len(AXES)):
            here = pos(p, 2)
            exchanged(p, 2, lambda o: far.at[p, (here + 4 - o) % 4])
            at = core * nb + pos(p, 0) * first + pos(p, 1) * second
            strip = pl.ds(pl.multiple_of(at, second), second)
            total[p, strip, :] = (far[p, 0] + far[p, 1]) + (far[p, 2] + far[p, 3])
            own = total.at[p, strip, :]
            exchange(p, 3, lambda j: own, lambda o: own)

    def strip_of(p, level, o):
        one = (pos(p, 0) + (4 - o if level == 4 else 0)) % 4
        if level == 4:
            return total.at[
                p, pl.ds(pl.multiple_of(core * nb + one * first, first), first), :]
        two = (pos(p, 1) + 4 - o) % 4
        at = core * nb + one * first + two * second
        return total.at[p, pl.ds(pl.multiple_of(at, second), second), :]

    def gather_one():
        for p in range(len(AXES)):
            exchanged(p, 3, lambda o: strip_of(p, 3, o))
            own = strip_of(p, 4, 0)
            exchange(p, 4, lambda j: own, lambda o: own)

    def gather_two():
        for p in range(len(AXES)):
            exchanged(p, 4, lambda o: strip_of(p, 4, o))
            own = cut(total, p, core, nb)
            remote(own, own, rsent.at[p, 16], rrecv.at[p, 16], peer["k"])

    def turn():
        for p in range(len(AXES)):
            here = cut(total, p, 1 - core, nb)
            remote(here, here, rsent.at[p, 16], rrecv.at[p, 16], peer["k"], False).wait_recv()
        last = len(AXES) - 1
        cross = jnp.concatenate(
            [total[last, :nb, wide - 128 :], total[last, nb:, wide - 128 :]], axis=1)
        keep = lax.broadcasted_iota(jnp.int32, (nb, nb), 0) <= lax.broadcasted_iota(
            jnp.int32, (nb, nb), 1)
        one = jnp.where(keep, factor_ref[0], 0.0)
        two = jnp.where(keep, factor_ref[1], 0.0)
        for p in range(len(AXES)):
            count = min(per, groups - p * per)
            at = pl.ds(p * wide, count * 128)
            s0 = total[p, :nb, : count * 128]
            c0 = dot(one, s0)
            s1 = total[p, nb:, : count * 128] - dot(cross, c0)
            c1 = dot(two, s1)
            proj[:nb, at] = s0
            proj[nb:, at] = s1
            value = jnp.concatenate([tall[p * per + i] for i in range(count)], axis=1)
            value = value - (dot(panel_ref[0], c0) + dot(panel_ref[1], c1))
            high, low = split(value)
            parts[:rows, at] = high
            parts[rows:, at] = low


    own = pltpu.make_async_copy(m_ref, slot(HOME), local.at[0])

    def compute(g, begin, count):
        b, dy = g
        _, c = source(row, col, (0, b, dy, 0))
        q = [name for name, _ in order].index(g)
        if begin == 0:
            for d in OFFSETS:
                if group(d) == g:
                    shared(d)
            if g == group(HOME):
                own.wait()
            if q >= made.shape[0]:
                stores[q - made.shape[0]].wait()
        where = q % made.shape[0]

        def unit(n, carry):
            at = pl.ds(pl.multiple_of(n * tile, tile), tile)
            m = full[c, :, at]
            high, low = split(m)
            both = jnp.dot(parts[...], high, preferred_element_type=F32)
            rest = jnp.dot(parts[:rows, :], low, preferred_element_type=F32)
            made[where, :, at] = both[:rows] + (both[rows:] + rest)
            line[...] += m[:, :128] + m[:, 128:]
            return carry

        lax.fori_loop(begin, begin + count, unit, 0)
        if begin + count == tiles:
            span = made.shape[2]
            store = pltpu.make_async_copy(
                made.at[where], out_ref.at[:, pl.ds(pl.multiple_of(c * span, span), span)],
                outsem.at[q])
            store.start()
            stores.append(store)

    def some(count):
        while count and todo:
            g, begin = todo.pop(0)
            take = min(count, tiles - begin)
            compute(g, begin, take)
            count -= take
            if begin + take < tiles:
                todo.insert(0, (g, begin + take))

    spread()
    own.start()
    line[...] = jnp.zeros_like(line)
    steps = [partial, pair, level_one, level_two, level_three, gather_one, gather_two, turn]
    tick = 0
    for t, plan in enumerate(PLAN):
        for half in range(HALVES):
            for step, d, n in plan:
                arrive(d, half)
                send(step, d, n, half)
            if t == 0 and half == 0:
                share(HOME)
            for at, action in zip(TICKS, steps):
                if at == tick:
                    action()
            if tick >= TICKS[-1]:
                some(BATCH)
            tick += 1
        if t:
            for _, _, n in PLAN[t - 1]:
                for half in range(HALVES):
                    arrive(n, half)
                share(n)
        todo.extend((g, 0) for g, last in order if last == t - 1)
    for _, _, n in PLAN[-1]:
        for half in range(HALVES):
            arrive(n, half)
        share(n)
    todo.extend((g, 0) for g, last in order if last == len(PLAN) - 1)
    some(len(order) * tiles)
    lanes = jnp.transpose(dot(proj[...], line[...]))
    sums = jnp.sum(lanes, axis=0, keepdims=True) / jnp.sqrt(F32(groups * full.shape[2]))
    wsum_ref[0:1, :] = sums[:, :nb]
    wsum_ref[1:2, :] = sums[:, nb:]
    for copy in started:
        copy.wait_send()
    for copy in stores[-made.shape[0] :]:
        copy.wait()


def per_device(basis, merge_coef, panels, factors):
    depth, span = merge_coef.shape
    groups = lax.axis_size("col")
    rows = basis.shape[0] // groups
    inner = basis.shape[1] * groups
    cols = span * groups
    nb = panels.shape[2]
    wide = (groups // len(AXES) + 1) * 128
    sems = pltpu.SemaphoreType.DMA
    vmem = lambda *shape: pltpu.VMEM(shape, F32)
    n = len(AXES)
    return pl.pallas_call(
        kernel,
        out_shape=(
            jax.ShapeDtypeStruct((rows, cols), F32),
            jax.ShapeDtypeStruct((2, nb), F32),
        ),
        in_specs=[pl.BlockSpec(memory_space=pltpu.VMEM)] * 4,
        out_specs=(pl.BlockSpec(memory_space=pl.ANY), pl.BlockSpec(memory_space=pltpu.VMEM)),
        scratch_shapes=[
            vmem(groups, inner, span),
            pltpu.VMEM((2 * rows, inner), BF16),
            vmem(groups // 2, rows, span),
            vmem(inner, 128),
            vmem(groups, rows, 128),
            vmem(n, 2 * nb, wide),
            vmem(n, nb, wide),
            vmem(n, nb, wide),
            vmem(n, 3, nb // 4, wide),
            vmem(n, nb // 4, wide),
            vmem(n, 3, nb // 16, wide),
            vmem(n, nb // 16, wide),
            vmem(n, 4, nb // 16, wide),
            vmem(n, 2 * nb, wide),
            vmem(2 * nb, inner),
            sems((len(OFFSETS), HALVES)),
            sems((len(OFFSETS), HALVES)),
            sems((len(OFFSETS),)),
            sems((len(OFFSETS),)),
            sems((2,)),
            sems((groups,)),
            sems((groups - 1,)),
            sems((groups - 1,)),
            sems((n, 17)),
            sems((n, 17)),
        ],
        compiler_params=pltpu.CompilerParams(
            collective_id=0, has_side_effects=True, vmem_limit_bytes=60 * 2**20
        ),
        cost_estimate=pl.CostEstimate(
            flops=6 * rows * inner * cols, bytes_accessed=4 * rows * cols, transcendentals=0
        ),
    )(merge_coef, basis, panels, factors)


def solution(mesh):
    return jax.shard_map(
        per_device,
        mesh=mesh,
        in_specs=(P("row", "col"), P("row", "col"), P(None, ("row", "col"), None), P()),
        out_specs=(P(("row", "col"), None), P()),
        check_vma=False,
    )
```

time: 293 us -> 130 us (0.44)
  waiting for transfers between devices: 166 us -> 0 us
  Pallas kernels: 79.8 us -> 121 us
  between operations: 14.1 us -> 0.65 us
  matrix products: 12.3 us -> 0 us
  starting transfers between devices: 7.53 us -> 0 us
  other arithmetic: 3.44 us -> 0 us
    psum x1 -> x0, waiting for transfers between devices: 153 us -> none  [per_device(): sums = lax.psum(sums, ('row', 'col'))]
    pallas_call x1, Pallas kernels: 79.8 us -> 121 us  [per_device(): pl.pallas_call(kernel, out_shape=(jax.ShapeDtypeStruct((rows, cols), F32)...]
    all_to_all x1 -> x0, waiting for transfers between devices: 13.1 us -> none  [per_device(): tall = lax.all_to_all(basis, 'col', split_axis=0, concat_axis=1, tiled=True)]
    dot_general x5 -> x0, matrix products: 12.3 us -> none  [matmul(): return jnp.dot(left, right, precision=precision, preferred_element_type=F32)]
    all_to_all x1 -> x0, starting transfers between devices: 7.49 us -> none  [per_device(): tall = lax.all_to_all(basis, 'col', split_axis=0, concat_axis=1, tiled=True)]
    unnamed x3 -> x4, local copies, waits for them, and re-layouts: 7.69 us -> 8.27 us
  transfers between devices with their start and end apart: 2 -> 0, of which waited for: 2 -> 0; matrix products, arithmetic and copies ran while one was open for 0% -> 0% of each run, Pallas kernels for 0% -> 0%
where the time goes in v3:
time: 130 us
  Pallas kernels  121 us (93%)
  local copies, waits for them, and re-layouts  8.27 us (6%)
    pallas_call x1, Pallas kernels, per_device(): pl.pallas_call(kernel, out_shape=(jax.ShapeDtypeStruct((rows, cols), F32)...  121 us
    unnamed x4, local copies, waits for them, and re-layouts  8.27 us

profile of v3, /device:TPU:1, one launch (start us, length us, event | category | flops | bytes accessed | tf_op | source)
XLA Modules:
  0.0 129.5 jit_solution(1419278265350455100)
XLA Ops:
  0.6 120.6 %shard_map.59 = (f32[256,8192]{1,0:T(8,128)}, f32[2,256]{1,0:T(2,128)}) custom-call(f32[64,1024]{1,0:T(8,128)} %m_ref.1, f32[2048,128]{1,0:T(8,128)} %basis_ref.1, f32[2,256,256]{2,1,0:T(8,128)} %panel_ref.1, f32[2,256,256]{2,1,0:T(8,128)} %factor_ref.1), custom_call_target="tpu_custom_call" | custom-call | flops 12884901888 | bytes 8388608 | tf_op jit(solution)/shard_map/pallas_call | solution.py:430
  121.2 0.0 copy-start
  121.3 7.7 %copy.8 = f32[256,8192]{1,0:T(8,128)} copy(f32[256,8192]{1,0:T(8,128)} %get-tuple-element.4) | data formatting | bytes 16777216
  128.9 0.0 copy-done
  128.9 0.6 copy.9
Async XLA Ops:
  121.2 7.7 %copy-start = (f32[2,256]{1,0:T(2,128)S(1)}, f32[2,256]{1,0:T(2,128)}, u32[]{:S(2)}) copy-start(f32[2,256]{1,0:T(2,128)} %get-tuple-element.5) | copy-start | bytes 6148

commit v4 on v3

--- a/solution.py
+++ b/solution.py
@@ -1,3 +1,5 @@
+import functools
+
 import jax
 import jax.numpy as jnp
 from jax import lax
@@ -27,7 +29,7 @@
     ((5, 63), (4, 60), (0, 56), (3, 63), (2, 21), (1, 10)),
     ((4, 26), (5, 59), (3, 61)),
 )
-HALVES = 2
+HALVES = 4
 
 
 def onward(d, step):
@@ -102,9 +104,15 @@
     return jnp.dot(left, right, precision=precision, preferred_element_type=F32)
 
 
+def dot3(left, right):
+    (a, b), (c, d) = split(left), split(right)
+    part = functools.partial(jnp.dot, preferred_element_type=F32)
+    return part(a, c) + (part(a, d) + part(b, c))
+
+
 AXES = (("z", "y", "x"), ("y", "x", "z"), ("x", "z", "y"))
-TICKS = (5, 6, 8, 9, 11, 12, 13, 15)
-BATCH = 5
+TICKS = (8, 8, 10, 14, 17, 20, 23, 26, 30)
+BATCH = 1
 
 
 def along(row, col, axis, step):
@@ -126,7 +134,7 @@
 
 def kernel(
     m_ref, basis_ref, panel_ref, factor_ref, out_ref, wsum_ref,
-    full, parts, made, line, tall, mine, twin, paired, near, nearest, mid, middle, far, total, proj,
+    full, parts, line, turned, tall, mine, twin, paired, near, nearest, mid, middle, far, total, proj,
     recv, sent, krecv, ksent, local, outsem, trecv, tsent, rrecv, rsent,
 ):
     row = lax.axis_index("row")
@@ -134,10 +142,10 @@
     _, _, core, _, _ = coords(row, col)
     depth = m_ref.shape[0]
     piece = depth // HALVES
-    tile = 256
+    tile = 512
     tiles = full.shape[2] // tile
     groups = full.shape[0]
-    rows = made.shape[1]
+    rows = out_ref.shape[0]
     nb = panel_ref.shape[2]
     peer = {step: neighbour(row, col, step) for step in STEPS + ("k",)}
 
@@ -148,8 +156,6 @@
     greeted += [peer["k"]]
     for device in greeted:
         pl.semaphore_signal(barrier, inc=1, device_id=device, device_id_type=MESH)
-    pl.semaphore_wait(barrier, len(greeted))
-
     started = []
     stores = []
     arrived = set()
@@ -201,7 +207,6 @@
     own_tall = pltpu.make_async_copy(block(col), tall.at[col], local.at[1])
 
     def spread():
-        own_tall.start()
         for o in range(1, groups):
             j = (col + o) % groups
             remote(block(j), tall.at[col], tsent.at[o - 1], trecv.at[o - 1], (row, j))
@@ -210,20 +215,25 @@
     wide = total.shape[2]
     per = wide // 128
 
-    def partial():
-        turned = jnp.transpose(jnp.concatenate([panel_ref[0], panel_ref[1]], axis=1))
-        cross = dot(turned[nb:], panel_ref[0])
+    def begin():
+        value = jnp.transpose(jnp.concatenate([panel_ref[0], panel_ref[1]], axis=1))
+        turned[...] = value
+        cross = dot3(value[nb:], panel_ref[0])
         last = len(AXES) - 1
         mine[last, :nb, wide - 128 :] = cross[:, :128]
         mine[last, nb:, wide - 128 :] = cross[:, 128:]
+
+    def landed():
         own_tall.wait()
         for o in range(1, groups):
             here = tall.at[(col + groups - o) % groups]
             remote(here, here, tsent.at[o - 1], trecv.at[o - 1], peer["k"], False).wait_recv()
+
+    def partial():
         for p in range(len(AXES)):
             count = min(per, groups - p * per)
             value = jnp.concatenate([tall[p * per + i] for i in range(count)], axis=1)
-            mine[p, :, : count * 128] = dot(turned, value)
+            mine[p, :, : count * 128] = dot3(turned[...], value)
             other = pl.ds(pl.multiple_of((1 - core) * nb, nb), nb)
             remote(mine.at[p, other], twin.at[p], rsent.at[p, 0], rrecv.at[p, 0], peer["k"])
 
@@ -320,13 +330,13 @@
             count = min(per, groups - p * per)
             at = pl.ds(p * wide, count * 128)
             s0 = total[p, :nb, : count * 128]
-            c0 = dot(one, s0)
-            s1 = total[p, nb:, : count * 128] - dot(cross, c0)
-            c1 = dot(two, s1)
+            c0 = dot3(one, s0)
+            s1 = total[p, nb:, : count * 128] - dot3(cross, c0)
+            c1 = dot3(two, s1)
             proj[:nb, at] = s0
             proj[nb:, at] = s1
             value = jnp.concatenate([tall[p * per + i] for i in range(count)], axis=1)
-            value = value - (dot(panel_ref[0], c0) + dot(panel_ref[1], c1))
+            value = value - (dot3(panel_ref[0], c0) + dot3(panel_ref[1], c1))
             high, low = split(value)
             parts[:rows, at] = high
             parts[rows:, at] = low
@@ -344,9 +354,6 @@
                     shared(d)
             if g == group(HOME):
                 own.wait()
-            if q >= made.shape[0]:
-                stores[q - made.shape[0]].wait()
-        where = q % made.shape[0]
 
         def unit(n, carry):
             at = pl.ds(pl.multiple_of(n * tile, tile), tile)
@@ -354,18 +361,11 @@
             high, low = split(m)
             both = jnp.dot(parts[...], high, preferred_element_type=F32)
             rest = jnp.dot(parts[:rows, :], low, preferred_element_type=F32)
-            made[where, :, at] = both[:rows] + (both[rows:] + rest)
-            line[...] += m[:, :128] + m[:, 128:]
+            out_ref[:, pl.ds(pl.multiple_of(c * full.shape[2] + n * tile, tile), tile)] = both[:rows] + (both[rows:] + rest)
+            line[...] += (m[:, :128] + m[:, 128:256]) + (m[:, 256:384] + m[:, 384:])
             return carry
 
         lax.fori_loop(begin, begin + count, unit, 0)
-        if begin + count == tiles:
-            span = made.shape[2]
-            store = pltpu.make_async_copy(
-                made.at[where], out_ref.at[:, pl.ds(pl.multiple_of(c * span, span), span)],
-                outsem.at[q])
-            store.start()
-            stores.append(store)
 
     def some(count):
         while count and todo:
@@ -376,20 +376,25 @@
             if begin + take < tiles:
                 todo.insert(0, (g, begin + take))
 
+    own.start()
+    own_tall.start()
+    line[...] = jnp.zeros_like(line)
+    begin()
+    pl.semaphore_wait(barrier, len(greeted))
     spread()
-    own.start()
-    line[...] = jnp.zeros_like(line)
-    steps = [partial, pair, level_one, level_two, level_three, gather_one, gather_two, turn]
+    steps = [landed, partial, pair, level_one, level_two, level_three, gather_one, gather_two, turn]
     tick = 0
     for t, plan in enumerate(PLAN):
         for half in range(HALVES):
+            if tick == TICKS[0]:
+                landed()
             for step, d, n in plan:
                 arrive(d, half)
                 send(step, d, n, half)
             if t == 0 and half == 0:
                 share(HOME)
             for at, action in zip(TICKS, steps):
-                if at == tick:
+                if at == tick and action is not landed:
                     action()
             if tick >= TICKS[-1]:
                 some(BATCH)
@@ -400,6 +405,7 @@
                     arrive(n, half)
                 share(n)
         todo.extend((g, 0) for g, last in order if last == t - 1)
+    some(len(order) * tiles)
     for _, _, n in PLAN[-1]:
         for half in range(HALVES):
             arrive(n, half)
@@ -412,8 +418,6 @@
     wsum_ref[1:2, :] = sums[:, nb:]
     for copy in started:
         copy.wait_send()
-    for copy in stores[-made.shape[0] :]:
-        copy.wait()
 
 
 def per_device(basis, merge_coef, panels, factors):
@@ -430,16 +434,16 @@
     return pl.pallas_call(
         kernel,
         out_shape=(
-            jax.ShapeDtypeStruct((rows, cols), F32),
-            jax.ShapeDtypeStruct((2, nb), F32),
+            pltpu.VMEM((rows, cols), F32),
+            pltpu.VMEM((2, nb), F32),
         ),
         in_specs=[pl.BlockSpec(memory_space=pltpu.VMEM)] * 4,
-        out_specs=(pl.BlockSpec(memory_space=pl.ANY), pl.BlockSpec(memory_space=pltpu.VMEM)),
+        out_specs=(pl.BlockSpec(memory_space=pltpu.VMEM), pl.BlockSpec(memory_space=pltpu.VMEM)),
         scratch_shapes=[
             vmem(groups, inner, span),
             pltpu.VMEM((2 * rows, inner), BF16),
-            vmem(groups // 2, rows, span),
             vmem(inner, 128),
+            vmem(2 * nb, rows),
             vmem(groups, rows, 128),
             vmem(n, 2 * nb, wide),
             vmem(n, nb, wide),
@@ -463,7 +467,7 @@
             sems((n, 17)),
         ],
         compiler_params=pltpu.CompilerParams(
-            collective_id=0, has_side_effects=True, vmem_limit_bytes=60 * 2**20
+            collective_id=0, has_side_effects=True, vmem_limit_bytes=54 * 2**20
         ),
         cost_estimate=pl.CostEstimate(
             flops=6 * rows * inner * cols, bytes_accessed=4 * rows * cols, transcendentals=0

time: 130 us -> 117 us (0.900)
  Pallas kernels: 121 us -> 113 us
  local copies, waits for them, and re-layouts: 8.27 us -> 3.98 us
    pallas_call x1, Pallas kernels: 121 us -> 113 us  [per_device(): pl.pallas_call(kernel, out_shape=(pltpu.VMEM((rows, cols), F32), pltpu.VM...]
    unnamed x4 -> x2, local copies, waits for them, and re-layouts: 8.27 us -> 3.98 us
where the time goes in v4:
time: 117 us
  Pallas kernels  113 us (97%)
  local copies, waits for them, and re-layouts  3.98 us (3%)
    pallas_call x1, Pallas kernels, per_device(): pl.pallas_call(kernel, out_shape=(pltpu.VMEM((rows, cols), F32), pltpu.VM...  113 us
    unnamed x2, local copies, waits for them, and re-layouts  3.98 us

profile of v4, /device:TPU:1, one launch (start us, length us, event | category | flops | bytes accessed | tf_op | source)
XLA Modules:
  0.0 117.2 jit_solution(17793700304677964266)
XLA Ops:
  0.6 112.6 %shard_map.59 = (f32[256,8192]{1,0:T(8,128)S(1)}, f32[2,256]{1,0:T(2,128)S(1)}) custom-call(f32[64,1024]{1,0:T(8,128)} %m_ref.1, f32[2048,128]{1,0:T(8,128)} %basis_ref.1, f32[2,256,256]{2,1,0:T(8,128)} %panel_ref.1, f32[2,256,256]{2,1,0:T(8,128)} %factor_ref.1), custom_call_target="tpu_custom_call" | custom-call | flops 12884901888 | bytes 8388608 | tf_op jit(solution)/shard_map/pallas_call | solution.py:434
  113.2 3.4 %copy.8 = f32[256,8192]{1,0:T(8,128)} copy(f32[256,8192]{1,0:T(8,128)S(1)} %get-tuple-element.2) | data formatting | bytes 16777216
  116.6 0.6 copy.9

commit v5 on v4

--- a/solution.py
+++ b/solution.py
@@ -112,6 +112,8 @@
 
 AXES = (("z", "y", "x"), ("y", "x", "z"), ("x", "z", "y"))
 TICKS = (8, 8, 10, 14, 17, 20, 23, 26, 30)
+TURNS = (2, 0, 1)
+STAGGER = 1
 BATCH = 1
 
 
@@ -229,8 +231,8 @@
             here = tall.at[(col + groups - o) % groups]
             remote(here, here, tsent.at[o - 1], trecv.at[o - 1], peer["k"], False).wait_recv()
 
-    def partial():
-        for p in range(len(AXES)):
+    def partial(parts_now):
+        for p in parts_now:
             count = min(per, groups - p * per)
             value = jnp.concatenate([tall[p * per + i] for i in range(count)], axis=1)
             mine[p, :, : count * 128] = dot3(turned[...], value)
@@ -259,23 +261,23 @@
 
     first, second = nb // 4, nb // 16
 
-    def pair():
-        for p in range(len(AXES)):
+    def pair(parts_now):
+        for p in parts_now:
             remote(twin.at[p], twin.at[p], rsent.at[p, 0], rrecv.at[p, 0], peer["k"],
                    False).wait_recv()
             keep = pl.ds(pl.multiple_of(core * nb, nb), nb)
             paired[p] = mine[p, keep, :] + twin[p]
             exchange(p, 0, lambda j: cut(paired, p, j, first), lambda o: near.at[p, o - 1])
 
-    def level_one():
-        for p in range(len(AXES)):
+    def level_one(parts_now):
+        for p in parts_now:
             exchanged(p, 0, lambda o: near.at[p, o - 1])
             keep = pl.ds(pl.multiple_of(pos(p, 0) * first, first), first)
             nearest[p] = (paired[p, keep, :] + near[p, 0]) + (near[p, 1] + near[p, 2])
             exchange(p, 1, lambda j: cut(nearest, p, j, second), lambda o: mid.at[p, o - 1])
 
-    def level_two():
-        for p in range(len(AXES)):
+    def level_two(parts_now):
+        for p in parts_now:
             exchanged(p, 1, lambda o: mid.at[p, o - 1])
             keep = pl.ds(pl.multiple_of(pos(p, 1) * second, second), second)
             value = (nearest[p, keep, :] + mid[p, 0]) + (mid[p, 1] + mid[p, 2])
@@ -284,8 +286,8 @@
             here = pos(p, 2)
             exchange(p, 2, lambda j: middle.at[p], lambda o: far.at[p, here])
 
-    def level_three():
-        for p in range(len(AXES)):
+    def level_three(parts_now):
+        for p in parts_now:
             here = pos(p, 2)
             exchanged(p, 2, lambda o: far.at[p, (here + 4 - o) % 4])
             at = core * nb + pos(p, 0) * first + pos(p, 1) * second
@@ -303,20 +305,20 @@
         at = core * nb + one * first + two * second
         return total.at[p, pl.ds(pl.multiple_of(at, second), second), :]
 
-    def gather_one():
-        for p in range(len(AXES)):
+    def gather_one(parts_now):
+        for p in parts_now:
             exchanged(p, 3, lambda o: strip_of(p, 3, o))
             own = strip_of(p, 4, 0)
             exchange(p, 4, lambda j: own, lambda o: own)
 
-    def gather_two():
-        for p in range(len(AXES)):
+    def gather_two(parts_now):
+        for p in parts_now:
             exchanged(p, 4, lambda o: strip_of(p, 4, o))
             own = cut(total, p, core, nb)
             remote(own, own, rsent.at[p, 16], rrecv.at[p, 16], peer["k"])
 
-    def turn():
-        for p in range(len(AXES)):
+    def turn(parts_now):
+        for p in parts_now:
             here = cut(total, p, 1 - core, nb)
             remote(here, here, rsent.at[p, 16], rrecv.at[p, 16], peer["k"], False).wait_recv()
         last = len(AXES) - 1
@@ -326,7 +328,7 @@
             jnp.int32, (nb, nb), 1)
         one = jnp.where(keep, factor_ref[0], 0.0)
         two = jnp.where(keep, factor_ref[1], 0.0)
-        for p in range(len(AXES)):
+        for p in parts_now:
             count = min(per, groups - p * per)
             at = pl.ds(p * wide, count * 128)
             s0 = total[p, :nb, : count * 128]
@@ -382,7 +384,7 @@
     begin()
     pl.semaphore_wait(barrier, len(greeted))
     spread()
-    steps = [landed, partial, pair, level_one, level_two, level_three, gather_one, gather_two, turn]
+    steps = [partial, pair, level_one, level_two, level_three, gather_one, gather_two, turn]
     tick = 0
     for t, plan in enumerate(PLAN):
         for half in range(HALVES):
@@ -393,10 +395,11 @@
                 send(step, d, n, half)
             if t == 0 and half == 0:
                 share(HOME)
-            for at, action in zip(TICKS, steps):
-                if at == tick and action is not landed:
-                    action()
-            if tick >= TICKS[-1]:
+            for at, action in zip(TICKS[1:], steps):
+                for i, p in enumerate(TURNS):
+                    if at + i * STAGGER == tick:
+                        action((p,))
+            if tick >= TICKS[-1] + (len(TURNS) - 1) * STAGGER:
                 some(BATCH)
             tick += 1
         if t:

time: 117 us -> 115 us (0.983)
  Pallas kernels: 113 us -> 110 us
    pallas_call x1, Pallas kernels: 113 us -> 110 us  [per_device(): pl.pallas_call(kernel, out_shape=(pltpu.VMEM((rows, cols), F32), pltpu.VM...]
where the time goes in v5:
time: 115 us
  Pallas kernels  110 us (96%)
  local copies, waits for them, and re-layouts  3.98 us (3%)
    pallas_call x1, Pallas kernels, per_device(): pl.pallas_call(kernel, out_shape=(pltpu.VMEM((rows, cols), F32), pltpu.VM...  110 us
    unnamed x2, local copies, waits for them, and re-layouts  3.98 us

profile of v5, /device:TPU:1, one launch (start us, length us, event | category | flops | bytes accessed | tf_op | source)
XLA Modules:
  0.0 114.8 jit_solution(6664232798521502619)
XLA Ops:
  0.6 110.2 %shard_map.59 = (f32[256,8192]{1,0:T(8,128)S(1)}, f32[2,256]{1,0:T(2,128)S(1)}) custom-call(f32[64,1024]{1,0:T(8,128)} %m_ref.1, f32[2048,128]{1,0:T(8,128)} %basis_ref.1, f32[2,256,256]{2,1,0:T(8,128)} %panel_ref.1, f32[2,256,256]{2,1,0:T(8,128)} %factor_ref.1), custom_call_target="tpu_custom_call" | custom-call | flops 12884901888 | bytes 8388608 | tf_op jit(solution)/shard_map/pallas_call | solution.py:437
  110.9 3.4 %copy.8 = f32[256,8192]{1,0:T(8,128)} copy(f32[256,8192]{1,0:T(8,128)S(1)} %get-tuple-element.2) | data formatting | bytes 16777216
  114.3 0.6 copy.9

commit v6 on v5

--- a/solution.py
+++ b/solution.py
@@ -195,12 +195,16 @@
         i, here = INDEX[n], slot(n, 0, half)
         remote(here, here, sent.at[i, half], recv.at[i, half], peer["k"], False).wait_recv()
 
-    def share(d):
-        remote(held(d), slot(d), ksent.at[INDEX[d]], krecv.at[INDEX[d]], peer["k"])
+    final = {n for _, _, n in PLAN[-1]}
+
+    def share(d, half=None):
+        i, at = INDEX[d], half or 0
+        remote(held(d, half), slot(d, 0, half), ksent.at[i, at], krecv.at[i, at], peer["k"])
 
     def shared(d):
-        i, here = INDEX[d], slot(d, 1)
-        remote(here, here, ksent.at[i], krecv.at[i], peer["k"], False).wait_recv()
+        for half in range(HALVES) if d in final else (None,):
+            i, at, here = INDEX[d], half or 0, slot(d, 1, half)
+            remote(here, here, ksent.at[i, at], krecv.at[i, at], peer["k"], False).wait_recv()
 
 
     def block(j):
@@ -409,10 +413,10 @@
                 share(n)
         todo.extend((g, 0) for g, last in order if last == t - 1)
     some(len(order) * tiles)
-    for _, _, n in PLAN[-1]:
-        for half in range(HALVES):
+    for half in range(HALVES):
+        for _, _, n in PLAN[-1]:
             arrive(n, half)
-        share(n)
+            share(n, half)
     todo.extend((g, 0) for g, last in order if last == len(PLAN) - 1)
     some(len(order) * tiles)
     lanes = jnp.transpose(dot(proj[...], line[...]))
@@ -460,8 +464,8 @@
             vmem(2 * nb, inner),
             sems((len(OFFSETS), HALVES)),
             sems((len(OFFSETS), HALVES)),
-            sems((len(OFFSETS),)),
-            sems((len(OFFSETS),)),
+            sems((len(OFFSETS), HALVES)),
+            sems((len(OFFSETS), HALVES)),
             sems((2,)),
             sems((groups,)),
             sems((groups - 1,)),

time: 115 us -> 118 us (1.026)
  Pallas kernels: 110 us -> 113 us
    pallas_call x1, Pallas kernels: 110 us -> 113 us  [per_device(): pl.pallas_call(kernel, out_shape=(pltpu.VMEM((rows, cols), F32), pltpu.VM...]
where the time goes in v6:
time: 118 us; the launch traced here: 117 us
  Pallas kernels  113 us (96%)
  local copies, waits for them, and re-layouts  3.98 us (3%)
    pallas_call x1, Pallas kernels, per_device(): pl.pallas_call(kernel, out_shape=(pltpu.VMEM((rows, cols), F32), pltpu.VM...  113 us
    unnamed x2, local copies, waits for them, and re-layouts  3.98 us

profile of v6, /device:TPU:1, one launch (start us, length us, event | category | flops | bytes accessed | tf_op | source)
XLA Modules:
  0.0 117.5 jit_solution(2002481066011666895)
XLA Ops:
  0.6 112.8 %shard_map.59 = (f32[256,8192]{1,0:T(8,128)S(1)}, f32[2,256]{1,0:T(2,128)S(1)}) custom-call(f32[64,1024]{1,0:T(8,128)} %m_ref.1, f32[2048,128]{1,0:T(8,128)} %basis_ref.1, f32[2,256,256]{2,1,0:T(8,128)} %panel_ref.1, f32[2,256,256]{2,1,0:T(8,128)} %factor_ref.1), custom_call_target="tpu_custom_call" | custom-call | flops 12884901888 | bytes 8388608 | tf_op jit(solution)/shard_map/pallas_call | solution.py:441
  113.5 3.4 %copy.8 = f32[256,8192]{1,0:T(8,128)} copy(f32[256,8192]{1,0:T(8,128)S(1)} %get-tuple-element.2) | data formatting | bytes 16777216
  116.9 0.6 copy.9
